TPU v7x, 256 devices: a whole 4x4x8 slice. The times are simulated.
256 devices in a mesh: req: 16 (over z, core), seq: 16 (over y, x).
Axes of the slice: x: 4, y: 4, z: 8, core: 2. Of those that a mesh axis runs over, the one named last changes fastest.
Arguments:
- kv_pool: float32 [16, 768, 2, 16, 512], P('req', 'seq'), may hold values from -10 to 10
- page_owner: int32 [4, 16, 192], P(None, 'req'), may hold values from 0 to 15, as said below
- page_slot: int32 [4, 16, 192], P(None, 'req'), may hold values from 0 to 47
- lengths: int32 [4, 16], P(None, 'req'), may hold values from 16 to 3072, as said below
- queries: float32 [4, 16, 4, 16, 256], P(None, 'req'), may hold values from -100 to 100
- gates: bfloat16 [4, 16, 4, 16, 256], P(None, 'req'), may hold values from -6 to 6
- new_kv: float32 [4, 16, 4, 2, 2, 256], P(None, 'req'), may hold values from -8 to 8
- tokens: bfloat16 [4, 16, 4, 2048], P(None, 'req'), may hold values from -6 to 6
- attn_gain: float32 [2048], replicated, may hold values from 0.1 to 1.9
- out_heads: bfloat16 [16, 256, 2048], P('seq'), may hold values from -0.09375 to 0.09375
- w_query_key: bfloat16 [2048, 16, 2, 128], P(None, 'seq'), may hold values from -0.125 to 0.125
- w_value_gate: bfloat16 [2048, 32, 2, 128], P(None, 'seq'), may hold values from -0.125 to 0.125
- w_beta_decay: bfloat16 [2048, 2, 32], P(None, None, 'seq'), may hold values from -0.125 to 0.125
- decay_scale: float32 [32], P('seq'), may hold values from 0.02 to 2
- dt_bias: float32 [32], P('seq'), may hold values from -2 to 2
- delta_gain: float32 [128], replicated, may hold values from 0.1 to 1.9
- w_delta_out: bfloat16 [32, 128, 2048], P('seq'), may hold values from -0.09375 to 0.09375
- prior_state: float32 [4, 16, 32, 128, 128], P(None, None, 'req', 'seq'), may hold values from -1.5 to 1.5
Outputs:
- layer_output: float32 [4, 16, 4, 2048], P(None, 'req', None, 'seq')
Inputs may be any that keep to these rules, and one draw needn't show every extreme that they name: In each request group g the pairs (page_owner, page_slot) over its 4 requests and 192 pages are all distinct, so each of the 16 owners holds exactly 48 of the group's pages and each share j // 12 of the sequence split covers exactly 48 pages. The pages of one group from one owner to one share number at most 6; every group has an owner and a share with exactly 6. `lengths`: both ends of the range occur in every draw.
All inputs are finite; a program needn't handle non-finite values.
Results may differ from a plain program's by a relative error of at most 0.005.
Values may be sent and summed in bfloat16 or wider, within the bound.
A program may use at most 128 MiB of HBM per device.

v0:
```python
import jax
import jax.numpy as jnp
from jax import lax
from jax.sharding import PartitionSpec as P

floor_score = -1e30
norm_eps = 1e-06
highest = lax.Precision.HIGHEST


def joined(part, axis, combine):
    gathered = jax.tree.map(lambda a: lax.all_gather(a, axis), part)

    def take(source):
        return jax.tree.map(lambda a: lax.dynamic_index_in_dim(a, source, 0, False), gathered)

    return lax.fori_loop(
        1, lax.axis_size(axis), lambda source, state: combine(state, take(source)), take(0)
    )


def rms_scale(values):
    return values * lax.rsqrt(jnp.mean(values * values, axis=-1, keepdims=True) + norm_eps)


def unit_rows(values):
    return values * lax.rsqrt(jnp.sum(values * values, axis=-1, keepdims=True) + norm_eps)


def join_parts(former, latter):
    ceiling = jnp.maximum(former[0], latter[0])
    factor_former = jnp.exp(former[0] - ceiling)
    factor_latter = jnp.exp(latter[0] - ceiling)
    summed = former[1] * factor_former + latter[1] * factor_latter
    weighted = former[2] * factor_former[..., None] + latter[2] * factor_latter[..., None]
    return (ceiling, summed, weighted)


def body(
    kv_pool,
    page_owner,
    page_slot,
    lengths,
    queries,
    gates,
    new_kv,
    tokens,
    attn_gain,
    out_heads,
    w_query_key,
    w_value_gate,
    w_beta_decay,
    decay_scale,
    dt_bias,
    delta_gain,
    w_delta_out,
    prior_state,
):
    seq_count = lax.axis_size("seq")
    device = lax.axis_index("seq")
    handed = lax.all_to_all(
        lax.all_to_all(
            prior_state.astype(jnp.bfloat16), "req", split_axis=1, concat_axis=2, tiled=True
        ),
        "seq",
        split_axis=2,
        concat_axis=3,
        tiled=True,
    ).astype(prior_state.dtype)[:, 0]
    own_pool = kv_pool[0]
    slot_count = own_pool.shape[0]
    owners = page_owner[:, 0]
    slot_table = page_slot[:, 0]
    requests = owners.shape[0]
    page_span = owners.shape[1]
    per_device = page_span // seq_count
    page_len = own_pool.shape[2]
    head_dim = queries.shape[-1]
    query_heads = queries.shape[-2]
    kv_heads = new_kv.shape[-2]
    grouped = query_heads // kv_heads
    step_count = queries.shape[2]
    flat_owner = owners.reshape(-1)
    flat_slot = slot_table.reshape(-1)
    flat_index = jnp.arange(requests * page_span, dtype=jnp.int32)
    capacity = 2 * slot_count // seq_count
    target = flat_index % page_span // per_device
    paired = flat_owner * seq_count + target
    matches = (
        paired[:, None] == jnp.arange(seq_count * seq_count, dtype=jnp.int32)[None, :]
    ).astype(jnp.int32)
    ranking = jnp.sum((jnp.cumsum(matches, axis=0) - matches) * matches, axis=1)
    bucket = target * capacity + ranking
    chosen = (bucket[None, :] == jnp.arange(seq_count * capacity, dtype=jnp.int32)[:, None]) & (
        flat_owner == device
    )[None, :]
    source_slot = jnp.sum(jnp.where(chosen, flat_slot[None, :], 0), axis=1)
    filled = jnp.any(chosen, axis=1)
    outgoing = jnp.where(filled[:, None, None, None], own_pool[source_slot], 0.0)
    outgoing = outgoing.reshape((seq_count, capacity) + own_pool.shape[1:])
    arrived = lax.all_to_all(outgoing, "seq", split_axis=0, concat_axis=0, tiled=True)
    arrived = arrived.reshape((seq_count * capacity,) + own_pool.shape[1:])
    local_owner = lax.dynamic_slice_in_dim(owners, device * per_device, per_device, 1)
    local_rank = lax.dynamic_slice_in_dim(
        ranking.reshape(requests, page_span), device * per_device, per_device, 1
    )
    page_rows = arrived[(local_owner * capacity + local_rank).reshape(-1)]
    page_order = jnp.arange(requests * per_device, dtype=jnp.int32)
    page_request = page_order // per_device
    page_start = (device * per_device + page_order % per_device) * page_len
    page_count = page_rows.shape[0]
    cache_keys = page_rows[:, 0].reshape(page_count, page_len, kv_heads, head_dim)
    cache_values = page_rows[:, 1].reshape(page_count, page_len, kv_heads, head_dim)
    grouped_queries = queries[:, 0].reshape(requests, step_count, kv_heads, grouped, head_dim)
    score_scale = head_dim ** (-0.5)
    page_queries = grouped_queries[page_request]
    scores = (
        jnp.einsum("nskgd,ntkd->nskgt", page_queries, cache_keys, precision=highest) * score_scale
    )
    positions = page_start[:, None] + jnp.arange(page_len, dtype=jnp.int32)[None, :]
    in_context = positions < lengths[:, 0][page_request][:, None]
    live_mask = in_context[:, None, None, None, :]
    page_top = jnp.max(jnp.where(live_mask, scores, floor_score), axis=-1)
    member = page_request[None, :] == jnp.arange(requests, dtype=jnp.int32)[:, None]
    request_top = jnp.max(
        jnp.where(member[:, :, None, None, None], page_top[None], floor_score), axis=1
    )
    weights = jnp.where(live_mask, jnp.exp(scores - request_top[page_request][..., None]), 0.0)
    member_float = member.astype(jnp.float32)
    request_sum = jnp.einsum(
        "rn,nskg->rskg", member_float, jnp.sum(weights, axis=-1), precision=highest
    )
    page_acc = jnp.einsum("nskgt,ntkd->nskgd", weights, cache_values, precision=highest)
    request_acc = jnp.einsum("rn,nskgd->rskgd", member_float, page_acc, precision=highest)
    request_top = request_top.reshape(requests, step_count, query_heads)
    request_sum = request_sum.reshape(requests, step_count, query_heads)
    request_acc = request_acc.reshape(requests, step_count, query_heads, head_dim)
    own_heads = out_heads.shape[0]
    merged = joined((request_top, request_sum, request_acc), "seq", join_parts)
    part_top = lax.dynamic_slice_in_dim(merged[0], device * own_heads, own_heads, 2)
    part_sum = lax.dynamic_slice_in_dim(merged[1], device * own_heads, own_heads, 2)
    part_acc = lax.dynamic_slice_in_dim(merged[2], device * own_heads, own_heads, 2)
    head_index = device * own_heads + jnp.arange(own_heads, dtype=jnp.int32)
    draft = new_kv[:, 0]
    draft_keys = draft[:, :, 0][:, :, head_index // grouped]
    draft_values = draft[:, :, 1][:, :, head_index // grouped]
    own_queries = lax.dynamic_slice_in_dim(queries[:, 0], device * own_heads, own_heads, 2)
    draft_scores = (
        jnp.einsum("rshd,ruhd->rshu", own_queries, draft_keys, precision=highest) * score_scale
    )
    causal = (jnp.arange(step_count)[:, None] >= jnp.arange(step_count)[None, :])[None, :, None, :]
    ceiling = jnp.maximum(part_top, jnp.max(jnp.where(causal, draft_scores, floor_score), axis=-1))
    carried = jnp.exp(part_top - ceiling)
    draft_weights = jnp.where(causal, jnp.exp(draft_scores - ceiling[..., None]), 0.0)
    denominator = part_sum * carried + jnp.sum(draft_weights, axis=-1)
    attended = part_acc * carried[..., None] + jnp.einsum(
        "rshu,ruhd->rshd", draft_weights, draft_values, precision=highest
    )
    attended = attended / denominator[..., None]
    own_gates = lax.dynamic_slice_in_dim(gates[:, 0], device * own_heads, own_heads, 2).astype(
        jnp.float32
    )
    gated_heads = (attended * jax.nn.sigmoid(own_gates)).astype(jnp.bfloat16)
    row_count = requests * step_count
    model_width = tokens.shape[-1]
    share_width = model_width // seq_count
    attn_part = jnp.dot(
        gated_heads.reshape(row_count, own_heads * head_dim),
        out_heads.reshape(own_heads * head_dim, model_width),
        preferred_element_type=jnp.float32,
    )
    residual_in = tokens[:, 0].reshape(row_count, model_width)
    stream = residual_in.astype(jnp.float32) + lax.psum(attn_part, "seq")
    normed = (rms_scale(stream) * attn_gain).astype(jnp.bfloat16)
    own_stream = lax.dynamic_slice_in_dim(stream, device * share_width, share_width, 1)
    key_local = w_query_key.shape[1]
    value_local = w_value_gate.shape[1]
    key_dim = w_query_key.shape[-1]
    value_dim = w_value_gate.shape[-1]
    head_ratio = value_local // key_local
    paired_proj = jnp.dot(
        normed,
        w_query_key.reshape(model_width, key_local * 2 * key_dim),
        preferred_element_type=jnp.float32,
    ).reshape(requests, step_count, key_local, 2, key_dim)
    delta_query = jnp.repeat(unit_rows(paired_proj[..., 0, :]), head_ratio, axis=2)
    delta_key = jnp.repeat(unit_rows(paired_proj[..., 1, :]), head_ratio, axis=2)
    value_proj = jnp.dot(
        normed,
        w_value_gate.reshape(model_width, value_local * 2 * value_dim),
        preferred_element_type=jnp.float32,
    ).reshape(requests, step_count, value_local, 2, value_dim)
    mixing = jnp.dot(
        normed,
        w_beta_decay.reshape(model_width, 2 * value_local),
        preferred_element_type=jnp.float32,
    ).reshape(requests, step_count, 2, value_local)
    beta_gate = jax.nn.sigmoid(mixing[:, :, 0])
    decay_rate = jnp.exp(-decay_scale * jax.nn.softplus(mixing[:, :, 1] + dt_bias))
    state_now = handed
    outputs = []
    for step_id in range(step_count):
        state_now = decay_rate[:, step_id, :, None, None] * state_now
        predicted = jnp.einsum("rhvk,rhk->rhv", state_now, delta_key[:, step_id], precision=highest)
        update = beta_gate[:, step_id, :, None] * (value_proj[:, step_id, :, 0] - predicted)
        state_now = state_now + update[..., :, None] * delta_key[:, step_id][..., None, :]
        outputs.append(
            jnp.einsum("rhvk,rhk->rhv", state_now, delta_query[:, step_id], precision=highest)
            * key_dim ** (-0.5)
        )
    readout = jnp.stack(outputs, axis=1)
    normalized = (rms_scale(readout) * delta_gain * jax.nn.silu(value_proj[..., 1, :])).astype(
        jnp.bfloat16
    )
    out_part = jnp.dot(
        normalized.reshape(row_count, value_local * value_dim),
        w_delta_out.reshape(value_local * value_dim, model_width),
        preferred_element_type=jnp.float32,
    )
    layer_sum = own_stream + lax.psum_scatter(out_part, "seq", scatter_dimension=1, tiled=True)
    return layer_sum.reshape(requests, 1, step_count, share_width)


def solution(mesh):
    return jax.shard_map(
        body,
        mesh=mesh,
        in_specs=(
            P("req", "seq", None, None, None),
            P(None, "req", None),
            P(None, "req", None),
            P(None, "req"),
            P(None, "req", None, None, None),
            P(None, "req", None, None, None),
            P(None, "req", None, None, None, None),
            P(None, "req", None, None),
            P(),
            P("seq", None, None),
            P(None, "seq", None, None),
            P(None, "seq", None, None),
            P(None, None, "seq"),
            P("seq"),
            P("seq"),
            P(),
            P("seq", None, None),
            P(None, None, "req", "seq", None),
        ),
        out_specs=P(None, "req", None, "seq"),
        check_vma=False,
    )
```

profile of v0, /device:TPU:1, one launch (start us, length us, event | category | flops | bytes accessed | tf_op | source)
XLA Modules:
  0.0 464.0 jit_solution(10900948446429253907)
XLA Ops:
  11.5 3.6 gather_fusion
  15.1 5.9 %broadcast_select_fusion = f32[16,6,2,16,512]{4,3,2,1,0:T(8,128)} fusion(f32[16,6,2,16,512]{4,3,2,1,0:T(8,128)} %bitcast.317, pred[16,6]{1,0:T(8,128)(4,1)S(1)} %broadcast_in_dim.138), kind=kLoop, calls=%fused_computation.16 | loop fusion | flops 1572864 | bytes 12583008 | tf_op jit(solution)/shard_map/jit(_where)/select_n | solution.py:99
  21.1 7.8 %all-to-all-start = ((f32[16,6,2,16,512]{4,3,2,1,0:T(8,128)}), f32[16,6,2,16,512]{4,3,2,1,0:T(8,128)}, u32[]{:S(2)}, u32[]{:S(2)}) async-start(f32[16,6,2,16,512]{4,3,2,1,0:T(8,128)} %broadcast_select_fusion), calls=%async_computation | async-start | bytes 12582912 | tf_op jit(solution)/shard_map/all_to_all | solution.py:101
  29.2 2.4 gather_fusion.2
  32.3 2.5 compare_select_fusion.4
  34.9 86.2 %all-to-all-done = f32[16,6,2,16,512]{4,3,2,1,0:T(8,128)} async-done(((f32[16,6,2,16,512]{4,3,2,1,0:T(8,128)}), f32[16,6,2,16,512]{4,3,2,1,0:T(8,128)}, u32[]{:S(2)}, u32[]{:S(2)}) %all-to-all-start) | async-done | bytes 6291488 | tf_op jit(solution)/shard_map/all_to_all | solution.py:101
  121.1 5.2 %gather_fusion.1 = f32[48,2,16,512]{3,2,1,0:T(8,128)} fusion(f32[96,2,16,512]{3,2,1,0:T(8,128)} %bitcast.15, s32[1024]{0:T(1024)S(1)} %pad_clamp_fusion.1), kind=kCustom, calls=%fused_computation.1 | custom fusion | bytes 6291648 | tf_op jit(solution)/shard_map/gather | solution.py:107
  126.4 4.1 fusion.121
  130.5 3.1 reshape_squeeze.11
  133.6 7.1 %fusion.8 = (f32[48,4,2,8]{3,1,2,0:T(4,128)}, f32[48,2,16,4,8]{2,4,3,1,0:T(8,128)}) fusion(pred[48,16]{1,0:T(8,128)(4,1)S(1)} %add_compare_fusion, f32[48,4,2,8,256]{4,3,2,1,0:T(8,128)} %gather_fusion.2, f32[48,16,2,256,1]{3,2,1,0,4:T(2,128)} %bitcast.319), kind=kOutput, calls=%fused_computation.21 | convolution fusion | flops 151139328 | bytes 4928256 | tf_op jit(solution)/shard_map/nskgd,ntkd->nskgt/dot_general | solution.py:118
  143.2 3.1 reshape_squeeze.13
  146.3 4.9 %convolution_bitcast_fusion = f32[48,4,2,8,256]{4,3,1,2,0:T(8,128)S(1)} fusion(f32[48,16,2,256,1]{3,2,1,0,4:T(2,128)} %bitcast.320, f32[48,2,16,4,8]{2,4,3,1,0:T(8,128)} %get-tuple-element.293, f32[48,4,2,8]{3,1,2,0:T(4,128)} %gather_fusion.3, pred[48,16]{1,0:T(8,128)(4,1)S(1)} %add_compare_fusion), kind=kOutput, calls=%fused_computation.17 | convolution fusion | flops 151093248 | bytes 4928256 | tf_op jit(solution)/shard_map/nskgt,ntkd->nskgd/dot_general | solution.py:133
  151.2 2.9 fusion.3
  156.7 10.3 %all-to-all-start.1 = ((bf16[4,16,2,8,128]{4,3,2,0,1:T(8,128)(2,1)}), bf16[4,16,2,8,128]{4,3,2,0,1:T(8,128)(2,1)}, u32[]{:S(2)}, u32[]{:S(2)}) async-start(bf16[4,16,2,8,128]{4,3,2,0,1:T(8,128)(2,1)} %copy.393), calls=%async_computation.1 | async-start | bytes 524288 | tf_op jit(solution)/shard_map/all_to_all | solution.py:62
  170.5 8.3 %all-to-all-done.1 = bf16[4,16,2,8,128]{4,3,2,0,1:T(8,128)(2,1)} async-done(((bf16[4,16,2,8,128]{4,3,2,0,1:T(8,128)(2,1)}), bf16[4,16,2,8,128]{4,3,2,0,1:T(8,128)(2,1)}, u32[]{:S(2)}, u32[]{:S(2)}) %all-to-all-start.1) | async-done | bytes 262176 | tf_op jit(solution)/shard_map/all_to_all | solution.py:62
  180.6 5.4 %all-to-all-start.2 = ((bf16[4,1,32,8,128]{4,3,0,1,2:T(8,128)(2,1)}), bf16[4,1,32,8,128]{4,3,0,1,2:T(8,128)(2,1)}, u32[]{:S(2)}, u32[]{:S(2)}) async-start(bf16[4,1,32,8,128]{4,3,0,1,2:T(8,128)(2,1)} %copy.269), calls=%async_computation.2 | async-start | bytes 524288 | tf_op jit(solution)/shard_map/all_to_all | solution.py:61
  186.1 2.4 fusion.18
  188.9 20.2 %all-gather = f32[64,4,16]{2,1,0:T(4,128)S(1)} all-gather(f32[4,4,16]{2,1,0:T(4,128)S(1)} %copy.256), channel_id=2, replica_groups=mesh['req'=16,'seq'=16] {'seq'}, dimensions={0}, use_global_device_ids=true | all-gather | bytes 17408 | tf_op jit(solution)/shard_map/all_gather | solution.py:12
  209.1 18.0 %all_gather.9 = f32[16,4,4,16]{3,2,1,0:T(4,128)S(1)} all-gather(f32[1,4,4,16]{3,2,1,0:T(4,128)S(1)} %all_gather_reshape.7), channel_id=1, replica_groups=mesh['req'=16,'seq'=16] {'seq'}, dimensions={0}, use_global_device_ids=true | all-gather | bytes 17408 | tf_op jit(solution)/shard_map/all_gather | solution.py:12
  228.7 27.7 %while.21 = (s32[]{:T(128)}, f32[4,4,16]{2,1,0:T(4,128)S(1)}, f32[4,4,16]{2,1,0:T(4,128)S(1)}, f32[4,4,16,256]{3,2,1,0:T(8,128)S(1)}, f32[16,4,4,16]{3,2,1,0:T(4...) while((s32[]{:T(128)}, f32[4,4,16]{2,1,0:T(4,128)S(1)}, ...), condition=%wide.region_9.10_spmd, body=%wide.region_8.9_spmd.sunk | while | flops 198149 | bytes 796823 | solution.py:17
  260.6 2.1 fusion.24
  262.8 2.4 copy.402
  265.2 2.3 copy.275
  267.5 4.1 reshape.612
  271.7 4.0 copy.274
  277.4 79.5 %all-reduce.2.cloned.1.call-done = f32[16,2048]{1,0:T(8,128)} async-done(((f32[16,2048]{1,0:T(8,128)}), f32[16,2048]{1,0:T(8,128)}) %all-reduce.2.cloned.1.call-update) | async-done | bytes 131088 | tf_op jit(solution)/shard_map/psum | solution.py:173
  360.8 2.3 fusion.62
  370.8 2.1 fusion.40
  373.0 2.2 fusion.61
  375.5 2.3 fusion.38
  377.9 2.4 fusion.33
  381.5 74.7 %reduce-scatter.2.cloned.1.call-done = f32[16,128]{1,0:T(8,128)} async-done(((f32[16,2048]{1,0:T(8,128)}), f32[16,128]{1,0:T(8,128)}) %reduce-scatter.2.cloned.1.call-update) | async-done | bytes 8208 | tf_op jit(solution)/shard_map/reduce_scatter | solution.py:220
  (193 shorter events, 66.1 us)
Async XLA Ops:
  6.5 5.0 %copy-start = (f32[1,48,2,16,512]{4,3,2,1,0:T(8,128)S(1)}, f32[1,48,2,16,512]{4,3,2,1,0:T(8,128)}, u32[]{:S(2)}) copy-start(f32[1,48,2,16,512]{4,3,2,1,0:T(8,128)} %param.20) | copy-start | bytes 9437188
  7.9 1.0 copy-start.2
  8.9 2.0 copy-start.8
  8.9 2.1 copy-start.12
  21.1 8.2 %copy-start.1 = (f32[4,1,4,16,256]{4,3,2,1,0:T(8,128)S(1)}, f32[4,1,4,16,256]{4,3,2,1,0:T(8,128)}, u32[]{:S(2)}) copy-start(f32[4,1,4,16,256]{4,3,2,1,0:T(8,128)} %param.24) | copy-start | bytes 786436
  21.1 100.1 %all-to-all-start = ((f32[16,6,2,16,512]{4,3,2,1,0:T(8,128)}), f32[16,6,2,16,512]{4,3,2,1,0:T(8,128)}, u32[]{:S(2)}, u32[]{:S(2)}) async-start(f32[16,6,2,16,512]{4,3,2,1,0:T(8,128)} %broadcast_select_fusion), calls=%async_computation | async-start | bytes 12582912 | tf_op jit(solution)/shard_map/all_to_all | solution.py:101
  28.8 198.9 %all-gather.3.cloned.1.call-start = ((), (), s32[]{:S(2)}) async-start(), calls=%async_computation.4 | async-start | bytes 4456448 | tf_op jit(solution)/shard_map/all_gather | solution.py:12
  29.2 2.4 copy-start.11
  151.2 17.3 %copy-start.7 = (f32[4,1,4,2,2,256]{5,4,3,2,1,0:T(2,128)S(1)}, f32[4,1,4,2,2,256]{5,4,3,2,1,0:T(2,128)}, u32[]{:S(2)}) copy-start(f32[4,1,4,2,2,256]{5,4,3,2,1,0:T(2,128)} %param.26) | copy-start | bytes 196612
  156.7 22.1 %all-to-all-start.1 = ((bf16[4,16,2,8,128]{4,3,2,0,1:T(8,128)(2,1)}), bf16[4,16,2,8,128]{4,3,2,0,1:T(8,128)(2,1)}, u32[]{:S(2)}, u32[]{:S(2)}) async-start(bf16[4,16,2,8,128]{4,3,2,0,1:T(8,128)(2,1)} %copy.393), calls=%async_computation.1 | async-start | bytes 524288 | tf_op jit(solution)/shard_map/all_to_all | solution.py:62
  168.5 17.5 %copy-start.13 = (pred[4,4]{0,1:T(4,128)(4,1)}, pred[4,4]{0,1:T(4,128)(4,1)S(1)}, u32[]{:S(2)}) copy-start(pred[4,4]{0,1:T(4,128)(4,1)S(1)} %iota_compare_fusion.4) | copy-start | bytes 52
  180.6 95.1 %all-to-all-start.2 = ((bf16[4,1,32,8,128]{4,3,0,1,2:T(8,128)(2,1)}), bf16[4,1,32,8,128]{4,3,0,1,2:T(8,128)(2,1)}, u32[]{:S(2)}, u32[]{:S(2)}) async-start(bf16[4,1,32,8,128]{4,3,0,1,2:T(8,128)(2,1)} %copy.269), calls=%async_computation.2 | async-start | bytes 524288 | tf_op jit(solution)/shard_map/all_to_all | solution.py:61
  186.0 170.8 %all-reduce.2.cloned.1.call-start = ((), (), s32[]{:S(2)}) async-start(), calls=%async_computation.5 | async-start | bytes 262144 | tf_op jit(solution)/shard_map/psum | solution.py:173
  227.1 0.6 copy-start.5
  256.4 6.3 %copy-start.6 = (bf16[4,1,4,2048]{3,2,1,0:T(4,128)(2,1)S(1)}, bf16[4,1,4,2048]{3,2,1,0:T(4,128)(2,1)}, u32[]{:S(2)}) copy-start(bf16[4,1,4,2048]{3,2,1,0:T(4,128)(2,1)} %param.27) | copy-start | bytes 196612
  262.7 193.5 %reduce-scatter.2.cloned.1.call-start = ((), (), s32[]{:S(2)}) async-start(), calls=%async_computation.6 | async-start | bytes 139264 | tf_op jit(solution)/shard_map/reduce_scatter | solution.py:220
  262.8 4.7 %copy-start.9 = (bf16[2048,2,2]{0,2,1:T(2,128)(2,1)S(1)}, bf16[2048,2,2]{0,2,1:T(2,128)(2,1)}, u32[]{:S(2)}) copy-start(bf16[2048,2,2]{0,2,1:T(2,128)(2,1)} %param.32) | copy-start | bytes 49156
  262.8 4.7 %copy-start.16 = (f32[2]{0:T(128)S(1)}, f32[2]{0:T(128)}, u32[]{:S(2)}) copy-start(f32[2]{0:T(128)} %param.33) | copy-start | bytes 28
  271.7 86.2 %copy-start.10 = (f32[2048]{0:T(1024)S(1)}, f32[2048]{0:T(1024)}, u32[]{:S(2)}) copy-start(f32[2048]{0:T(1024)} %param.28) | copy-start | bytes 24580
  275.6 84.6 %copy-start.15 = (f32[2]{0:T(128)S(1)}, f32[2]{0:T(128)}, u32[]{:S(2)}) copy-start(f32[2]{0:T(128)} %param.34) | copy-start | bytes 28
  360.8 4.4 copy-start.4
  375.3 5.2 %copy-start.14 = (f32[128]{0:T(128)S(1)}, f32[128]{0:T(128)}, u32[]{:S(2)}) copy-start(f32[128]{0:T(128)} %param.35) | copy-start | bytes 1540
  375.5 5.1 %copy-start.3 = (bf16[2,128,2048]{2,1,0:T(8,128)(2,1)S(1)}, bf16[2,128,2048]{2,1,0:T(8,128)(2,1)}, u32[]{:S(2)}) copy-start(bf16[2,128,2048]{2,1,0:T(8,128)(2,1)} %param.36) | copy-start | bytes 3145732
Sparse Core Ops, SparseCore 0:
  155.0 60.0 all-gather.2
  262.8 93.9 all-reduce.1
  381.6 74.5 reduce-scatter.1
where the time goes:
time: 467 us; the launch traced here: 464 us
  waiting for transfers between devices  249 us (53%)
  local copies, waits for them, and re-layouts  51.5 us (11%)
  other arithmetic  47 us (10%)
  matrix products  41 us (9%)
  blocking collectives  38.2 us (8%)
  starting transfers between devices  23.6 us (5%)
  between operations  13.6 us (3%)
    all_to_all x1, waiting for transfers between devices, body(): lax.all_to_all(outgoing, 'seq', split_axis=0, concat_axis=0, tiled=True)  86.2 us
    psum x1, waiting for transfers between devices, body(): stream = residual_in.astype(jnp.float32) + lax.psum(attn_part, 'seq')  79.5 us
    reduce_scatter x1, waiting for transfers between devices, body(): lax.psum_scatter(out_part, 'seq', scatter_dimension=1, tiled=True)  74.7 us
    all_gather x2, blocking collectives, joined(): gathered = jax.tree.map(lambda a: lax.all_gather(a, axis), part)  38.2 us
    add x15, other arithmetic, join_parts(): former[2] * factor_former[..., None] + latter[2] * factor_latter[..., None]  16.4 us
    add x15, other arithmetic, join_parts(): summed = former[1] * factor_former + latter[1] * factor_latter  10.9 us
    all_to_all x1, starting transfers between devices, body(): lax.all_to_all(prior_state.astype(jnp.bfloat16), 'req', split_axis=1, con...  10.3 us
  transfers between devices with their start and end apart: 6, of which 4 were waited for; matrix products, arithmetic and copies ran while one was open for 14% of the time, Pallas kernels for 0%

commit v1 on v0

v1 whole, which is shorter than its diff:
```python
import jax
import jax.numpy as jnp
from jax import lax
from jax.experimental import pallas as pl
from jax.experimental.pallas import tpu as pltpu
from jax.sharding import PartitionSpec as P

floor_score = -1e30
norm_eps = 1e-06
MESH = pl.DeviceIdType.MESH
f32 = jnp.float32
bf16 = jnp.bfloat16

GROUP = 16
REQS = 4
STEPS = 4
ROWS = REQS * STEPS
SLOTS = 48
PAGE = 16
TOKENS = SLOTS * PAGE
PAGES = 192
HD = 256
D = 2048
SHARE = 128
KVH = 2
PER_KV = 8
MSG = HD + 128
OFFSETS = [(y, x) for y in range(4) for x in range(4) if y or x]
FAR_FIRST = sorted(OFFSETS, key=lambda o: -(min(o[0], 4 - o[0]) + min(o[1], 4 - o[1])))
PLACES = (1, 0, 3, 2, 6, 5, 7, 4)
ALONG_X = [(0, 2), (0, 1), (0, 3)]
ALONG_Y = [(2, 0), (1, 0), (3, 0)]


def dot(a, b):
    return jnp.dot(a, b, preferred_element_type=f32)


def dot_t(a, b):
    return lax.dot_general(a, b, (((1,), (1,)), ((), ())), preferred_element_type=f32)


def iota(shape, axis):
    return lax.broadcasted_iota(jnp.int32, shape, axis)


def shifted(x, by):
    return jnp.concatenate([x[-by:], x[:-by]], axis=0) if by else x


def kernel(
    kv_hbm, owner_hbm, slot_hbm, lengths, q_hbm, gates_hbm, new_hbm, tokens_hbm, gain_hbm, wo_hbm,
    wqk_hbm, wvg_hbm, wmix_hbm, decay_scale, dt_bias, dgain_hbm, wdo_hbm, state_hbm,
    out_ref,
    kv, owner, slot, q, gates, new, tokens, gain, wo, wqk, wvg, wmix, dgain, wdo, state,
    fq, fv, w_all, w_mix, s_out, s_in, m_out, m_in, a_out, a_in, x_out, x_in, stream,
    d_out, d_in, load_sem, send_sem, recv_sem, ready_sem,
):
    i = lax.axis_index("req")
    me = lax.axis_index("seq")

    loads = {}

    def load(name, src, dst):
        copy = pltpu.make_async_copy(src, dst, load_sem.at[len(loads)])
        copy.start()
        loads[name] = copy

    def rank(plane):
        level = 0
        for z, place in enumerate(PLACES):
            level = jnp.where(plane // 2 == z, place, level)
        return 2 * level + 1 - lax.rem(plane, 2)

    def peer(offset):
        y, x = offset
        return lax.rem(me // 4 + y, 4) * 4 + lax.rem(lax.rem(me, 4) + x, 4)

    my_rank = rank(i)
    barrier = pltpu.get_barrier_semaphore()

    def greet(where):
        pl.semaphore_signal(barrier, inc=1, device_id=where, device_id_type=MESH)

    def each_state_peer(use):
        for d in range(GROUP):
            use(d, lax.rem(i + d, GROUP))

    def each_state_source(use):
        for d in range(GROUP):
            source = lax.rem(me + d, GROUP)
            if d:
                use(source)
            else:

                @pl.when(i != me)
                def _():
                    use(source)

    for offset in FAR_FIRST:
        greet((i, peer(offset)))
    early_receiver = my_rank <= rank(me)

    @pl.when(early_receiver)
    def _():
        each_state_source(lambda source: greet((me, source)))

    def greet_later(d, g):
        @pl.when(rank(g) > my_rank)
        def _():
            greet((g, i))

    each_state_peer(greet_later)

    load("owner", owner_hbm, owner)
    load("slot", slot_hbm, slot)
    load("q", q_hbm.at[:, 0:128], q.at[0])
    load("q_more", q_hbm.at[:, 128:256], q.at[1])
    load("kv", kv_hbm, kv)
    load("state", state_hbm, state)
    load("gates", gates_hbm, gates)
    load("new", new_hbm, new)
    load("wo", wo_hbm, wo)
    load("tokens", tokens_hbm.at[:, 0], tokens)
    load("gain", gain_hbm, gain)
    load("wqk", wqk_hbm, wqk)
    load("wvg", wvg_hbm, wvg)
    load("wmix", wmix_hbm, wmix)
    load("dgain", dgain_hbm, dgain)
    load("wdo", wdo_hbm, wdo)

    loads["owner"].wait()
    loads["slot"].wait()
    page_at = iota((SLOTS, PAGES), 1)
    slot_at = iota((SLOTS, PAGES), 0)
    row_request = lax.rem(iota((SLOTS, 128), 1) // STEPS, REQS)
    counts = jnp.zeros((SLOTS, 128), f32)
    for r in range(REQS):
        live = jnp.clip(lengths[r] - page_at * PAGE, 0, PAGE)
        held = (owner[r] == me) & (slot[r] == slot_at)
        count = jnp.sum(jnp.where(held, live, 0).astype(f32), axis=1, keepdims=True)
        counts = jnp.where(row_request == r, count, counts)
    spread = (iota((SLOTS, TOKENS), 1) // PAGE == iota((SLOTS, TOKENS), 0)).astype(f32).astype(bf16)
    limit = lax.dot_general(
        counts.astype(bf16), spread, (((0,), (0,)), ((), ())), preferred_element_type=f32
    )
    in_page = lax.rem(iota((128, TOKENS), 1), PAGE).astype(f32)
    live_mask = in_page < limit

    def head_queries(h):
        halves = [q[half, pl.ds(h, ROWS, stride=GROUP), :] for half in range(2)]
        return jnp.concatenate(halves, axis=1) * (HD ** -0.5)

    loads["q"].wait()
    loads["q_more"].wait()
    loads["kv"].wait()
    stat_lane = iota((128, 128), 1)
    for k in range(KVH):
        queries = jnp.concatenate([head_queries(k * PER_KV + h) for h in range(PER_KV)], axis=0)
        q_hi = queries.astype(bf16)
        q_lo = (queries - q_hi.astype(f32)).astype(bf16)
        keys = kv[:, 0, :, k * HD : (k + 1) * HD].reshape(TOKENS, HD)
        k_hi = keys.astype(bf16)
        k_lo = (keys - k_hi.astype(f32)).astype(bf16)
        scores = dot_t(q_hi, k_hi) + (dot_t(q_lo, k_hi) + dot_t(q_hi, k_lo))
        scores = jnp.where(live_mask, scores, floor_score)
        top = jnp.max(scores, axis=1, keepdims=True).astype(bf16).astype(f32)
        weights = jnp.where(live_mask, jnp.exp(scores - top), 0.0).astype(bf16)
        total = jnp.sum(weights.astype(f32), axis=1, keepdims=True)
        values = kv[:, 1, :, k * HD : (k + 1) * HD].reshape(TOKENS, HD).astype(bf16)
        acc = dot(weights, values)
        total_hi = total.astype(bf16).astype(f32)
        stats = jnp.where(stat_lane == 0, top, jnp.where(stat_lane == 1, total_hi, total - total_hi))
        own = pl.ds(k * PER_KV, PER_KV)
        m_out[own, :, 0:HD] = acc.astype(bf16).reshape(PER_KV, ROWS, HD)
        m_out[own, :, HD:MSG] = stats.astype(bf16).reshape(PER_KV, ROWS, 128)

    own_state = (i == me).astype(jnp.int32)
    late_receiver = (my_rank > rank(me)).astype(jnp.int32)
    pl.semaphore_wait(barrier, GROUP + my_rank - own_state + GROUP * late_receiver)

    def send(src, dst, phase, where, sent_at=None):
        pltpu.make_async_remote_copy(
            src_ref=src,
            dst_ref=dst,
            send_sem=send_sem.at[phase if sent_at is None else sent_at],
            recv_sem=recv_sem.at[phase],
            device_id=where,
            device_id_type=MESH,
        ).start()

    def scatter(src, dst, phase):
        for n, offset in enumerate(FAR_FIRST):
            other = peer(offset)
            send(src.at[other], dst.at[n], phase, (i, other))

    def arrived(ref, phase):
        pltpu.make_async_copy(ref, ref, recv_sem.at[phase]).wait()

    def sent(ref, phase):
        pltpu.make_async_copy(ref, ref, send_sem.at[phase]).wait()

    scatter(m_out, m_in, 0)

    loads["state"].wait()
    for g in range(GROUP):
        s_out[g] = state[:, g].reshape(REQS * 2 * 8, 128).astype(bf16)

    def send_states(later):
        def one(g):
            @pl.when(rank(g) > my_rank if later else rank(g) < my_rank)
            def _():
                send(s_out.at[g], s_in.at[me], 1, (g, i))

        for d in range(GROUP):
            one(lax.rem(i + me + GROUP - d, GROUP))

    @pl.when(jnp.logical_not(early_receiver))
    def _():
        each_state_source(
            lambda source: pl.semaphore_signal(
                ready_sem, inc=1, device_id=(me, source), device_id_type=MESH
            )
        )

    send_states(False)

    @pl.when(i != me)
    def _():
        send(s_out.at[i], s_in.at[me], 1, (i, i), 5)

    @pl.when(i == me)
    def _():
        pltpu.make_async_copy(s_out.at[i], s_in.at[me], recv_sem.at[1]).start()

    loads["wqk"].wait()
    loads["wvg"].wait()
    chunk = 256

    def arrange(c, carry):
        rows = pl.ds(pl.multiple_of(c * chunk, chunk), chunk)
        fq[...] = wqk[pl.ds(pl.multiple_of(c * (2 * chunk), 2 * chunk), 2 * chunk), :].astype(f32)
        fv[...] = wvg[pl.ds(pl.multiple_of(c * (4 * chunk), 4 * chunk), 4 * chunk), :].astype(f32)
        for n in range(2):
            w_all[rows, n * 128 : (n + 1) * 128] = fq[pl.ds(n, chunk, stride=2), :].astype(bf16)
        for n in range(4):
            w_all[rows, (n + 2) * 128 : (n + 3) * 128] = fv[pl.ds(n, chunk, stride=4), :].astype(bf16)
        return carry

    lax.fori_loop(0, D // chunk, arrange, 0)
    loads["wmix"].wait()
    for n in range(2):
        w_mix[2 * n : 2 * n + 2, :] = wmix[n].astype(f32)

    loads["new"].wait()
    loads["gates"].wait()
    own_q = head_queries(me)
    low_kv = me < PER_KV

    def draft(component):
        both = new[:, component].astype(f32)
        return jnp.where(low_kv, both[:, 0], both[:, 1])

    draft_scores = lax.dot_general(
        own_q, draft(0), (((1,), (1,)), ((), ())),
        preferred_element_type=f32, precision=lax.Precision.HIGHEST,
    )
    row, col = iota((ROWS, ROWS), 0), iota((ROWS, ROWS), 1)
    causal = (row // STEPS == col // STEPS) & (col <= row)
    draft_scores = jnp.where(causal, draft_scores, floor_score)
    draft_top = jnp.max(draft_scores, axis=1, keepdims=True)
    draft_weights = jnp.where(causal, jnp.exp(draft_scores - draft_top), 0.0)
    draft_total = jnp.sum(draft_weights, axis=1, keepdims=True)
    draft_acc = lax.dot_general(
        draft_weights, draft(1), (((1,), (0,)), ((), ())),
        preferred_element_type=f32, precision=lax.Precision.HIGHEST,
    )
    own_gate = jnp.sum(
        jnp.where(iota((ROWS, GROUP, HD), 1) == me, gates[...].astype(f32), 0.0), axis=1
    )
    gate = jax.nn.sigmoid(own_gate)

    arrived(m_in, 0)
    parts = [m_out[me]] + [m_in[d] for d in range(GROUP - 1)]
    ceiling = draft_top
    for part in parts:
        ceiling = jnp.maximum(ceiling, part[:, HD : HD + 1].astype(f32))
    factor = jnp.exp(draft_top - ceiling)
    total = draft_total * factor
    acc = draft_acc * factor
    for part in parts:
        stats = part[:, HD:MSG].astype(f32)
        factor = jnp.exp(stats[:, 0:1] - ceiling)
        total = total + factor * (stats[:, 1:2] + stats[:, 2:3])
        acc = acc + factor * part[:, 0:HD].astype(f32)
    gated = (acc / total * gate).astype(bf16)

    loads["wo"].wait()
    halves = [slice(0, D // 2), slice(D // 2, D)]

    def send_half(src, dst, n, along, phase):
        for m, offset in enumerate(along):
            send(src.at[n], dst.at[n, m], phase, (i, peer(offset)))

    ways = (ALONG_X, ALONG_Y)
    sums = []
    for n in range(2):
        sums.append(dot(gated, wo[:, halves[n]]))
        a_out[n] = sums[n].astype(bf16)
        send_half(a_out, a_in, n, ways[n], 2 + n)
    @pl.when(my_rank < GROUP - 1)
    def _():
        pl.semaphore_wait(ready_sem, GROUP - 1 - my_rank)

    send_states(True)
    for n in range(2):
        arrived(a_in.at[n], 2 + n)
        sums[n] = sums[n] + (a_in[n, 0].astype(f32) + a_in[n, 1].astype(f32) + a_in[n, 2].astype(f32))
        x_out[n] = sums[n].astype(bf16)
        send_half(x_out, x_in, n, ways[1 - n], 6 + n)

    loads["tokens"].wait()
    own_tokens = tokens[...].astype(f32).reshape(ROWS, D)

    loads["gain"].wait()
    loads["dgain"].wait()
    loads["wdo"].wait()
    arrived(s_in, 1)

    handed = s_in[...].astype(f32).reshape(GROUP, REQS, 2, 8, 128)
    states = []
    for r in range(REQS):
        blocks = [handed[j, r, h] for h in range(2) for j in range(GROUP)]
        states.append(jnp.concatenate(blocks, axis=0).astype(bf16))

    squares = jnp.zeros((ROWS, 1), f32)
    proj = jnp.zeros((ROWS, 6 * 128), f32)
    mixes = [jnp.zeros((ROWS, 1), f32) for _ in range(4)]
    for n in range(2):
        arrived(x_in.at[n], 6 + n)
        x = own_tokens[:, halves[n]] + (
            sums[n] + (x_in[n, 0].astype(f32) + x_in[n, 1].astype(f32) + x_in[n, 2].astype(f32))
        )
        stream[:, halves[n]] = x
        squares = squares + jnp.sum(x * x, axis=1, keepdims=True)
        y = (x * gain[:, halves[n]]).astype(bf16)
        proj = proj + dot(y, w_all[halves[n], :])
        y = y.astype(f32)
        for c in range(4):
            mixes[c] = mixes[c] + jnp.sum(y * w_mix[c : c + 1, halves[n]], axis=1, keepdims=True)
    scale = lax.rsqrt(squares * (1.0 / D) + norm_eps)
    proj = proj * scale
    mixes = [mix * scale for mix in mixes]

    def unit(x):
        return x * lax.rsqrt(jnp.sum(x * x, axis=1, keepdims=True) + norm_eps)

    dq = unit(proj[:, 0:128])
    dk = unit(proj[:, 128:256])
    value = jnp.concatenate([proj[:, 256:384], proj[:, 512:640]], axis=1)
    zgate = jnp.concatenate([proj[:, 384:512], proj[:, 640:768]], axis=1)
    high = iota((ROWS, 2 * 128), 1) >= 128
    beta = jnp.where(high, jax.nn.sigmoid(mixes[1]), jax.nn.sigmoid(mixes[0]))

    def decay_of(h):
        t = mixes[2 + h] + dt_bias[h]
        soft = jnp.maximum(t, 0.0) + jnp.log(1.0 + jnp.exp(-jnp.abs(t)))
        return jnp.exp(-decay_scale[h] * soft)

    decay = jnp.where(high, decay_of(1), decay_of(0))

    both = jnp.concatenate([dk, dq], axis=0).astype(bf16)
    row_of = lax.rem(iota((2 * ROWS, 2 * 128), 0) // STEPS, REQS)
    prior = jnp.zeros((2 * ROWS, 2 * 128), f32)
    for r in range(REQS):
        prior = jnp.where(row_of == r, dot_t(both, states[r]), prior)
    prior_k, prior_q = prior[:ROWS], prior[ROWS:]
    step = lax.rem(iota((ROWS, 2 * 128), 0), STEPS)
    ratio = [jnp.ones((ROWS, 2 * 128), f32), decay]
    for o in range(1, STEPS):
        ratio.append(decay * shifted(ratio[o], 1))
    whole = jnp.where(step == 0, ratio[1], jnp.where(step == 1, ratio[2], jnp.where(step == 2, ratio[3], ratio[4])))
    key_back = [shifted(dk, o) for o in range(STEPS)]
    beta_prior = beta * (value - whole * prior_k)
    coupling = [
        jnp.where(step >= o, beta * ratio[o] * jnp.sum(dk * key_back[o], axis=1, keepdims=True), 0.0)
        for o in range(1, STEPS)
    ]
    update = beta_prior
    for _ in range(STEPS - 1):
        following = beta_prior
        for o in range(1, STEPS):
            following = following - coupling[o - 1] * shifted(update, o)
        update = following
    readout = whole * prior_q
    for o in range(STEPS):
        reach = jnp.sum(dq * key_back[o], axis=1, keepdims=True)
        readout = readout + jnp.where(step >= o, ratio[o] * reach, 0.0) * shifted(update, o)
    readout = readout * (128 ** -0.5)

    def normal(x):
        return x * lax.rsqrt(jnp.mean(x * x, axis=1, keepdims=True) + norm_eps) * dgain[...]

    normalized = jnp.concatenate([normal(readout[:, :128]), normal(readout[:, 128:])], axis=1)
    normalized = (normalized * zgate * jax.nn.sigmoid(zgate)).astype(bf16)

    total = dot(normalized, wdo[...])
    for e in range(GROUP):
        d_out[e] = total[:, e * SHARE : (e + 1) * SHARE].astype(bf16)
    scatter(d_out, d_in, 4)
    own_lanes = pl.ds(pl.multiple_of(me * SHARE, SHARE), SHARE)
    result = stream[:, own_lanes] + d_out[me].astype(f32)
    sent(m_in, 0)
    sent(s_in.at[pl.ds(0, GROUP - 1)], 1)

    @pl.when(i != me)
    def _():
        sent(s_in.at[0], 5)

    for n in range(2):
        sent(a_in.at[n], 2 + n)
        sent(x_in.at[n], 6 + n)
    arrived(d_in, 4)
    for d in range(GROUP - 1):
        result = result + d_in[d].astype(f32)
    out_ref[...] = result
    sent(d_in, 4)


def body(
    kv_pool, page_owner, page_slot, lengths, queries, gates, new_kv, tokens, attn_gain, out_heads,
    w_query_key, w_value_gate, w_beta_decay, decay_scale, dt_bias, delta_gain, w_delta_out, prior_state,
):
    hbm = pl.BlockSpec(memory_space=pl.ANY)
    smem = pl.BlockSpec(memory_space=pltpu.SMEM)
    vmem = pltpu.VMEM
    operands = (
        (kv_pool.reshape(SLOTS, 2, PAGE, KVH * HD), hbm),
        (page_owner, hbm),
        (page_slot, hbm),
        (lengths.reshape(REQS), smem),
        (queries.reshape(ROWS * GROUP, HD), hbm),
        (gates.reshape(ROWS, GROUP, HD), hbm),
        (new_kv.reshape(ROWS, 2, KVH, HD), hbm),
        (tokens, hbm),
        (attn_gain.reshape(1, D), hbm),
        (out_heads.reshape(HD, D), hbm),
        (w_query_key.reshape(2 * D, 128), hbm),
        (w_value_gate.reshape(4 * D, 128), hbm),
        (w_beta_decay.transpose(1, 2, 0), hbm),
        (decay_scale, smem),
        (dt_bias, smem),
        (delta_gain.reshape(1, 128), hbm),
        (w_delta_out.reshape(2 * 128, D), hbm),
        (prior_state, hbm),
    )
    out = pl.pallas_call(
        kernel,
        out_shape=jax.ShapeDtypeStruct((ROWS, SHARE), f32),
        in_specs=[spec for _, spec in operands],
        out_specs=pl.BlockSpec(memory_space=pltpu.VMEM),
        scratch_shapes=[
            vmem((SLOTS, 2, PAGE, KVH * HD), f32),
            vmem((REQS, 1, PAGES), jnp.int32),
            vmem((REQS, 1, PAGES), jnp.int32),
            vmem((2, ROWS * GROUP, 128), f32),
            vmem((ROWS, GROUP, HD), bf16),
            vmem((ROWS, 2, KVH, HD), f32),
            vmem((REQS, STEPS, D), bf16),
            vmem((1, D), f32),
            vmem((HD, D), bf16),
            vmem((2 * D, 128), bf16),
            vmem((4 * D, 128), bf16),
            vmem((2, 2, D), bf16),
            vmem((1, 128), f32),
            vmem((2 * 128, D), bf16),
            vmem((REQS, GROUP, 2, 8, 128), f32),
            vmem((512, 128), f32),
            vmem((1024, 128), f32),
            vmem((D, 6 * 128), bf16),
            vmem((8, D), f32),
            vmem((GROUP, 64, 128), bf16),
            vmem((GROUP, 64, 128), bf16),
            vmem((GROUP, ROWS, MSG), bf16),
            vmem((GROUP - 1, ROWS, MSG), bf16),
            vmem((2, ROWS, D // 2), bf16),
            vmem((2, 3, ROWS, D // 2), bf16),
            vmem((2, ROWS, D // 2), bf16),
            vmem((2, 3, ROWS, D // 2), bf16),
            vmem((ROWS, D), f32),
            vmem((GROUP, ROWS, SHARE), bf16),
            vmem((GROUP - 1, ROWS, SHARE), bf16),
            pltpu.SemaphoreType.DMA((16,)),
            pltpu.SemaphoreType.DMA((8,)),
            pltpu.SemaphoreType.DMA((8,)),
            pltpu.SemaphoreType.REGULAR,
        ],
        compiler_params=pltpu.CompilerParams(
            collective_id=0, has_side_effects=True, vmem_limit_bytes=60 * 1024 * 1024
        ),
    )(*[value for value, _ in operands])
    return out.reshape(REQS, 1, STEPS, SHARE)


def solution(mesh):
    return jax.shard_map(
        body,
        mesh=mesh,
        in_specs=(
            P("req", "seq", None, None, None),
            P(None, "req", None),
            P(None, "req", None),
            P(None, "req"),
            P(None, "req", None, None, None),
            P(None, "req", None, None, None),
            P(None, "req", None, None, None, None),
            P(None, "req", None, None),
            P(),
            P("seq", None, None),
            P(None, "seq", None, None),
            P(None, "seq", None, None),
            P(None, None, "seq"),
            P("seq"),
            P("seq"),
            P(),
            P("seq", None, None),
            P(None, None, "req", "seq", None),
        ),
        out_specs=P(None, "req", None, "seq"),
        check_vma=False,
    )
```

time: 467 us -> 31.8 us (0.07)
  waiting for transfers between devices: 249 us -> 0 us
  local copies, waits for them, and re-layouts: 51.5 us -> 1.3 us
  other arithmetic: 47 us -> 0 us
  matrix products: 41 us -> 0 us
  blocking collectives: 38.2 us -> 0 us
  Pallas kernels: 0 us -> 30.3 us
  starting transfers between devices: 23.6 us -> 0 us
  between operations: 13.6 us -> 0.01 us
    all_to_all x3 -> x0, waiting for transfers between devices: 94.5 us -> none  [the longest x1 86.2 us: body(): lax.all_to_all(outgoing, 'seq', split_axis=0, concat_axis=0, tiled=True)]
    psum x1 -> x0, waiting for transfers between devices: 79.5 us -> none  [body(): stream = residual_in.astype(jnp.float32) + lax.psum(attn_part, 'seq')]
    reduce_scatter x1 -> x0, waiting for transfers between devices: 74.7 us -> none  [body(): lax.psum_scatter(out_part, 'seq', scatter_dimension=1, tiled=True)]
    dot_general x19 -> x0, matrix products: 41 us -> none  [the longest x4 8.36 us: body(): jnp.einsum('rhvk,rhk->rhv', state_now, delta_key[:, step_id], precision=h...]
    all_gather x2 -> x0, blocking collectives: 38.2 us -> none  [joined(): gathered = jax.tree.map(lambda a: lax.all_gather(a, axis), part)]
    pallas_call x0 -> x1, Pallas kernels: none -> 30.3 us  [body(): pl.pallas_call(kernel, out_shape=jax.ShapeDtypeStruct((ROWS, SHARE), f32)...]
    add x35 -> x0, other arithmetic: 28.8 us -> none  [the longest x15 16.4 us: join_parts(): former[2] * factor_former[..., None] + latter[2] * factor_latter[..., None]]
    all_to_all x3 -> x0, starting transfers between devices: 23.5 us -> none  [the longest x1 10.3 us: body(): lax.all_to_all(prior_state.astype(jnp.bfloat16), 'req', split_axis=1, con...]
  transfers between devices with their start and end apart: 6 -> 0, of which waited for: 4 -> 0; matrix products, arithmetic and copies ran while one was open for 14% -> 0% of each run, Pallas kernels for 0% -> 0%
where the time goes in v1:
time: 31.8 us; the launch traced here: 31.6 us
  Pallas kernels  30.3 us (95%)
  local copies, waits for them, and re-layouts  1.3 us (4%)
    pallas_call x1, Pallas kernels, body(): pl.pallas_call(kernel, out_shape=jax.ShapeDtypeStruct((ROWS, SHARE), f32)...  30.3 us
    unnamed x1, local copies, waits for them, and re-layouts  1.3 us

profile of v1, /device:TPU:1, one launch (start us, length us, event | category | flops | bytes accessed | tf_op | source)
XLA Modules:
  0.0 31.6 jit_solution(15493987697640666199)
XLA Ops:
  0.0 30.3 %shard_map.172 = f32[16,128]{1,0:T(8,128)} custom-call(f32[48,2,16,512]{3,2,1,0:T(8,128)} %bitcast.15, s32[4,1,192]{2,1,0:T(1,128)} %owner_hbm.1, s32[4,1,192]{2,1,0:T(1,128)} %slot_hbm.1, s32[4]{0:T(128)} %bitcast.26, f32[256,256]{1,0:T(8,128)} %bitcast.20, bf16[16,16,256]{2,1,0:T(8,128)(2,1)} %bitcast.21, f32[16,2,2,256]{3,2,1,0:T(2,128)} %bitcast.22, ...), custom_call_target="tpu_custom_call" | custom-call | tf_op jit(solution)/shard_map/pallas_call | solution.py:457
  30.3 1.3 %copy.21 = f32[4,1,4,128]{3,2,1,0:T(4,128)} copy(f32[4,1,4,128]{3,2,1,0:T(4,128)} %bitcast.23) | data formatting | bytes 16384

commit v2 on v1

v2 whole, which is shorter than its diff:
```python
import jax
import jax.numpy as jnp
from jax import lax
from jax.experimental import pallas as pl
from jax.experimental.pallas import tpu as pltpu
from jax.sharding import PartitionSpec as P

floor_score = -1e30
norm_eps = 1e-06
MESH = pl.DeviceIdType.MESH
f32 = jnp.float32
bf16 = jnp.bfloat16

GROUP = 16
REQS = 4
STEPS = 4
ROWS = REQS * STEPS
BOTH = 2 * ROWS
LEVELS = 8
SLOTS = 48
PAGE = 16
TOKENS = SLOTS * PAGE
PAGES = 192
HD = 256
D = 2048
SHARE = 128
KVH = 2
PER_KV = 8
MSG = HD + 128
OFFSETS = [(y, x) for y in range(4) for x in range(4) if y or x]
FAR_FIRST = sorted(OFFSETS, key=lambda o: -(min(o[0], 4 - o[0]) + min(o[1], 4 - o[1])))
PLACES = (1, 0, 3, 2, 6, 5, 7, 4)


def dot(a, b):
    return jnp.dot(a, b, preferred_element_type=f32)


def dot_t(a, b):
    return lax.dot_general(a, b, (((1,), (1,)), ((), ())), preferred_element_type=f32)


def iota(shape, axis):
    return lax.broadcasted_iota(jnp.int32, shape, axis)


def shifted(x, by):
    return jnp.concatenate([x[-by:], x[:-by]], axis=0) if by else x


def kernel(
    kv_hbm, owner_hbm, slot_hbm, lengths, q_hbm, gates_hbm, new_hbm, tokens_hbm, gain_hbm, wo_hbm,
    wqk_hbm, wvg_hbm, wmix_hbm, decay_scale, dt_bias, dgain_hbm, wdo_hbm, state_hbm,
    out_ref,
    kv, owner, slot, q, gates, new, tokens, gain, wo, wqk, wvg, wmix, dgain, wdo, state,
    fq, fv, w_all, w_mix, s_out, s_more, s_in, held_states, m_out, m_in, draft_out, gate_out, gate_in,
    a_out, a_in, x_out, x_in, d_out, d_in, base_out, base_in,
    load_sem, send_sem, recv_sem, ready_sem, go_sem,
):
    i = lax.axis_index("req")
    me = lax.axis_index("seq")
    z = i // 2
    core = lax.rem(i, 2)
    front = 2 * z + 1
    back = 2 * z
    on_front = core == 1
    on_back = core == 0

    copies = {}

    def plan(name, src, dst):
        copies[name] = pltpu.make_async_copy(src, dst, load_sem.at[len(copies)])

    own_lanes = pl.ds(pl.multiple_of(me * SHARE, SHARE), SHARE)
    plan("q", q_hbm.at[:, 0:128], q.at[0])
    plan("q_more", q_hbm.at[:, 128:256], q.at[1])
    for k in range(KVH):
        for part in range(2):
            lanes = slice(k * HD, (k + 1) * HD)
            plan(("keys", "values")[part] + str(k), kv_hbm.at[:, part, :, lanes], kv.at[k, part])
    plan("owner", owner_hbm, owner)
    plan("slot", slot_hbm, slot)
    for copy in copies.values():
        copy.start()

    def rank(level):
        place = 0
        for n, p in enumerate(PLACES):
            place = jnp.where(level == n, p, place)
        return place

    def peer(offset):
        y, x = offset
        return lax.rem(me // 4 + y, 4) * 4 + lax.rem(lax.rem(me, 4) + x, 4)

    my_rank = rank(z)
    barrier = pltpu.get_barrier_semaphore()

    def greet(where):
        pl.semaphore_signal(barrier, inc=1, device_id=where, device_id_type=MESH)

    def each_state_source(use):
        for d in range(GROUP):
            use((2 * (me // 2), lax.rem(me + d, GROUP)))

    for offset in FAR_FIRST:
        greet((front, peer(offset)))

    @pl.when(on_back)
    def _():
        greet((front, me))

    @pl.when(on_front)
    def _():
        for offset in FAR_FIRST:
            greet((back, peer(offset)))
        greet((back, me))

    early_receiver = on_front & (my_rank <= rank(me // 2))
    late_receiver = on_front & (my_rank > rank(me // 2))

    @pl.when(early_receiver)
    def _():
        each_state_source(greet)

    for d in range(1, LEVELS):
        level = lax.rem(z + d, LEVELS)

        @pl.when(on_back & (rank(level) > my_rank))
        def _():
            for c in range(2):
                greet((2 * level + 1, 2 * z + c))

    copies["owner"].wait()
    copies["slot"].wait()
    page_at = iota((SLOTS, PAGES), 1)
    slot_at = iota((SLOTS, PAGES), 0)
    row_request = lax.rem(iota((SLOTS, 128), 1) // STEPS, REQS)
    counts = jnp.zeros((SLOTS, 128), f32)
    for r in range(REQS):
        live = jnp.clip(lengths[r] - page_at * PAGE, 0, PAGE)
        held = (owner[r] == me) & (slot[r] == slot_at)
        count = jnp.sum(jnp.where(held, live, 0).astype(f32), axis=1, keepdims=True)
        counts = jnp.where(row_request == r, count, counts)
    in_page = iota((SLOTS, PAGE, 128), 1).astype(f32)
    live_mask = (in_page < counts[:, None, :]).reshape(TOKENS, 128)

    def head_queries(h):
        halves = [q[half, pl.ds(h, ROWS, stride=GROUP), :] for half in range(2)]
        return jnp.concatenate(halves, axis=1) * (HD ** -0.5)

    def part_stats(top, total):
        lane = iota((top.shape[0], 128), 1)
        total_hi = total.astype(bf16).astype(f32)
        stats = jnp.where(lane == 0, top, jnp.where(lane == 1, total_hi, total - total_hi))
        return stats.astype(bf16)

    plan("state", state_hbm, state)
    plan("gates", gates_hbm, gates)
    plan("new", new_hbm, new)
    plan("wqk", wqk_hbm, wqk)
    plan("wvg", wvg_hbm, wvg)
    plan("wmix", wmix_hbm, wmix)
    plan("wo", wo_hbm, wo)
    plan("tokens", tokens_hbm.at[:, 0, :, own_lanes], tokens.at[1])
    plan("gain", gain_hbm, gain)
    plan("dgain", dgain_hbm, dgain)
    plan("wdo", wdo_hbm, wdo)

    copies["q"].wait()
    copies["q_more"].wait()
    for k in range(KVH):
        queries = jnp.concatenate([head_queries(k * PER_KV + h) for h in range(PER_KV)], axis=0)
        q_hi = queries.astype(bf16)
        q_lo = (queries - q_hi.astype(f32)).astype(bf16)
        copies["keys" + str(k)].wait()
        keys = kv[k, 0].reshape(TOKENS, HD)
        k_hi = keys.astype(bf16)
        k_lo = (keys - k_hi.astype(f32)).astype(bf16)
        by_hi = dot_t(k_hi, jnp.concatenate([q_hi, q_lo], axis=0))
        scores = by_hi[:, :128] + (by_hi[:, 128:] + dot_t(k_lo, q_hi))
        scores = jnp.where(live_mask, scores, floor_score)
        top = jnp.max(scores, axis=0, keepdims=True).astype(bf16).astype(f32)
        weights = jnp.where(live_mask, jnp.exp(scores - top), 0.0).astype(bf16)
        total = jnp.sum(weights.astype(f32), axis=0, keepdims=True)
        copies["values" + str(k)].wait()
        values = kv[k, 1].reshape(TOKENS, HD).astype(bf16)
        own = pl.ds(k * PER_KV, PER_KV)
        acc = lax.dot_general(weights, values, (((0,), (0,)), ((), ())), preferred_element_type=f32)
        m_out[own, :, 0:HD] = acc.astype(bf16).reshape(PER_KV, ROWS, HD)
        total_hi = total.astype(bf16).astype(f32)
        sides = jnp.concatenate([top, total_hi, total - total_hi, jnp.zeros((125, 128), f32)], axis=0)
        m_out[own, :, HD:MSG] = sides.T.astype(bf16).reshape(PER_KV, ROWS, 128)

    for name in ("state", "gates", "new"):
        copies[name].start()

    @pl.when(on_front)
    def _():
        for name in ("wqk", "wvg", "wmix", "wo", "tokens", "gain", "dgain", "wdo"):
            copies[name].start()

    pl.semaphore_wait(
        barrier,
        jnp.where(
            on_front,
            2 * GROUP - 1 + GROUP * late_receiver.astype(jnp.int32),
            GROUP + 2 * (my_rank + 1),
        ),
    )

    def send(src, dst, phase, where, sent_at=None):
        pltpu.make_async_remote_copy(
            src_ref=src,
            dst_ref=dst,
            send_sem=send_sem.at[phase if sent_at is None else sent_at],
            recv_sem=recv_sem.at[phase],
            device_id=where,
            device_id_type=MESH,
        ).start()

    def arrived(ref, phase):
        pltpu.make_async_copy(ref, ref, recv_sem.at[phase]).wait()

    def sent(ref, phase):
        pltpu.make_async_copy(ref, ref, send_sem.at[phase]).wait()

    for n, offset in enumerate(FAR_FIRST):
        other = peer(offset)
        send(m_out.at[other], m_in.at[n, core], 0, (front, other))

    @pl.when(on_back)
    def _():
        send(m_out.at[me], m_in.at[GROUP - 1, 0], 0, (front, me))
        send(tokens_hbm.at[:, 0, :, own_lanes], tokens.at[0], 9, (front, me))

    @pl.when(late_receiver)
    def _():
        each_state_source(
            lambda source: pl.semaphore_signal(
                ready_sem, inc=1, device_id=source, device_id_type=MESH
            )
        )

    copies["new"].wait()
    copies["gates"].wait()
    own_q = head_queries(me)
    low_kv = me < PER_KV

    def draft(component):
        both = new[:, component].astype(f32)
        return jnp.where(low_kv, both[:, 0], both[:, 1])

    draft_scores = lax.dot_general(
        own_q, draft(0), (((1,), (1,)), ((), ())),
        preferred_element_type=f32, precision=lax.Precision.HIGHEST,
    )
    row, col = iota((ROWS, ROWS), 0), iota((ROWS, ROWS), 1)
    causal = (row // STEPS == col // STEPS) & (col <= row)
    draft_scores = jnp.where(causal, draft_scores, floor_score)
    draft_top = jnp.max(draft_scores, axis=1, keepdims=True).astype(bf16).astype(f32)
    draft_weights = jnp.where(causal, jnp.exp(draft_scores - draft_top), 0.0)
    draft_acc = lax.dot_general(
        draft_weights, draft(1), (((1,), (0,)), ((), ())),
        preferred_element_type=f32, precision=lax.Precision.HIGHEST,
    )
    draft_out[:, 0:HD] = draft_acc.astype(bf16)
    draft_out[:, HD:MSG] = part_stats(draft_top, jnp.sum(draft_weights, axis=1, keepdims=True))
    own_gate = jnp.sum(
        jnp.where(iota((ROWS, GROUP, HD), 1) == me, gates[...].astype(f32), 0.0), axis=1
    )
    gate_out[...] = own_gate.astype(bf16)

    @pl.when(on_back)
    def _():
        send(draft_out, m_in.at[GROUP, 0], 0, (front, me))
        send(gate_out, gate_in, 8, (front, me))

    copies["state"].wait()
    for g in range(GROUP):
        s_out[g] = state[:, g].reshape(REQS * 2 * 8, 128).astype(bf16)

    @pl.when(on_back)
    def _():
        def send_states(c, chosen):
            for d in range(LEVELS):
                level = lax.rem(z + me + LEVELS - d, LEVELS)

                @pl.when(chosen(rank(level)))
                def _():
                    send(
                        (s_out, s_more)[c].at[pl.ds(2 * level, 2)], s_in.at[me], 1, (2 * level + 1, 2 * z + c)
                    )

        send_states(0, lambda place: place <= my_rank)
        arrived(s_more, 5)
        send_states(1, lambda place: place <= my_rank)

        @pl.when(my_rank < LEVELS - 1)
        def _():
            pl.semaphore_wait(ready_sem, 2 * (LEVELS - 1 - my_rank))

        pl.semaphore_wait(go_sem, 1)
        for c in range(2):
            send_states(c, lambda place: place > my_rank)
        sent(s_out, 1)
        sent(s_more, 1)

    @pl.when(on_front)
    def _():
        send(s_out, s_more, 5, (back, me))

    @pl.when(on_back)
    def _():
        sent(m_in.at[:, 0], 0)
        sent(tokens.at[0], 9)
        sent(gate_in, 8)
        arrived(base_in, 10)
        arrived(d_in, 4)
        result = base_in[...]
        for n in range(GROUP):
            result = result + d_in[n].astype(f32)
        out_ref[...] = result

    @pl.when(on_front)
    def _():
        m_in[GROUP - 1, 1] = m_out[me]
        m_in[GROUP, 1] = draft_out[...]

        copies["wqk"].wait()
        copies["wvg"].wait()
        chunk = 256

        def arrange(c, carry):
            rows = pl.ds(pl.multiple_of(c * chunk, chunk), chunk)
            fq[...] = wqk[pl.ds(pl.multiple_of(c * (2 * chunk), 2 * chunk), 2 * chunk), :].astype(f32)
            fv[...] = wvg[pl.ds(pl.multiple_of(c * (4 * chunk), 4 * chunk), 4 * chunk), :].astype(f32)
            for n in range(2):
                w_all[rows, n * 128 : (n + 1) * 128] = fq[pl.ds(n, chunk, stride=2), :].astype(bf16)
            for n in range(4):
                w_all[rows, (n + 2) * 128 : (n + 3) * 128] = fv[pl.ds(n, chunk, stride=4), :].astype(bf16)
            return carry

        lax.fori_loop(0, D // chunk, arrange, 0)
        copies["wmix"].wait()
        for n in range(2):
            w_mix[2 * n : 2 * n + 2, :] = wmix[n].astype(f32)
        for name in ("wo", "tokens", "gain", "dgain", "wdo"):
            copies[name].wait()
        arrived(gate_in, 8)
        arrived(tokens.at[0], 9)
        gate = jax.nn.sigmoid(jnp.concatenate([gate_in[...], gate_out[...]], axis=0).astype(f32))

        arrived(m_in.at[pl.ds(0, GROUP)], 0)
        pl.semaphore_signal(go_sem, inc=1, device_id=(back, me), device_id_type=MESH)
        parts = [m_in[n].reshape(BOTH, MSG) for n in range(GROUP + 1)]
        ceiling = parts[0][:, HD : HD + 1].astype(f32)
        for part in parts[1:]:
            ceiling = jnp.maximum(ceiling, part[:, HD : HD + 1].astype(f32))
        total = jnp.zeros((BOTH, 1), f32)
        acc = jnp.zeros((BOTH, HD), f32)
        for part in parts:
            stats = part[:, HD:MSG].astype(f32)
            factor = jnp.exp(stats[:, 0:1] - ceiling)
            total = total + factor * (stats[:, 1:2] + stats[:, 2:3])
            acc = acc + factor * part[:, 0:HD].astype(f32)
        gated = (acc / total * gate).astype(bf16)

        total = dot(gated, wo[...])
        for e in range(GROUP):
            a_out[e] = total[:, e * SHARE : (e + 1) * SHARE].astype(bf16)
        for n, offset in enumerate(FAR_FIRST):
            other = peer(offset)
            send(a_out.at[other], a_in.at[n], 2, (front, other))
        stream = tokens[...].astype(f32).reshape(BOTH, SHARE) + a_out[me].astype(f32)
        arrived(a_in, 2)
        for n in range(GROUP - 1):
            stream = stream + a_in[n].astype(f32)

        own_x = (stream * gain[:, own_lanes]).astype(bf16)
        x_out[...] = own_x
        x_in[me] = own_x
        for offset in FAR_FIRST:
            send(x_out, x_in.at[me], 3, (front, peer(offset)))
        base_out[...] = stream[0:ROWS]
        send(base_out, base_in, 10, (back, me))

        arrived(s_in, 1)
        for g in range(2):
            for r in range(REQS):
                rows = s_in[:, g, r * 16 : (r + 1) * 16].astype(f32).reshape(GROUP, 2, 8, 128)
                blocks = [rows[j, h] for h in range(2) for j in range(GROUP)]
                held_states[g * REQS + r] = jnp.concatenate(blocks, axis=0).astype(bf16)

        arrived(x_in.at[pl.ds(0, GROUP - 1)], 3)
        y = jnp.concatenate([x_in[e] for e in range(GROUP)], axis=1)
        proj = dot(y, w_all[...])
        y = y.astype(f32)
        mixes = [jnp.sum(y * w_mix[c : c + 1], axis=1, keepdims=True) for c in range(4)]
        x = y / gain[...]
        squares = jnp.sum(x * x, axis=1, keepdims=True)
        scale = lax.rsqrt(squares * (1.0 / D) + norm_eps)
        proj = proj * scale
        mixes = [mix * scale for mix in mixes]

        def unit(x):
            return x * lax.rsqrt(jnp.sum(x * x, axis=1, keepdims=True) + norm_eps)

        dq = unit(proj[:, 0:128])
        dk = unit(proj[:, 128:256])
        value = jnp.concatenate([proj[:, 256:384], proj[:, 512:640]], axis=1)
        zgate = jnp.concatenate([proj[:, 384:512], proj[:, 640:768]], axis=1)
        wide = (BOTH, 2 * 128)
        high = iota(wide, 1) >= 128
        beta = jnp.where(high, jax.nn.sigmoid(mixes[1]), jax.nn.sigmoid(mixes[0]))

        def decay_of(h):
            t = mixes[2 + h] + dt_bias[h]
            soft = jnp.maximum(t, 0.0) + jnp.log(1.0 + jnp.exp(-jnp.abs(t)))
            return jnp.exp(-decay_scale[h] * soft)

        decay = jnp.where(high, decay_of(1), decay_of(0))

        both = jnp.concatenate([dk, dq], axis=0).astype(bf16)
        row_of = lax.rem(iota((2 * BOTH, 2 * 128), 0) // STEPS, 2 * REQS)
        prior = jnp.zeros((2 * BOTH, 2 * 128), f32)
        for r in range(2 * REQS):
            prior = jnp.where(row_of == r, dot_t(both, held_states[r]), prior)
        prior_k, prior_q = prior[:BOTH], prior[BOTH:]
        step = lax.rem(iota(wide, 0), STEPS)
        ratio = [jnp.ones(wide, f32), decay]
        for o in range(1, STEPS):
            ratio.append(decay * shifted(ratio[o], 1))
        whole = jnp.where(
            step == 0, ratio[1], jnp.where(step == 1, ratio[2], jnp.where(step == 2, ratio[3], ratio[4]))
        )
        key_back = [shifted(dk, o) for o in range(STEPS)]
        beta_prior = beta * (value - whole * prior_k)
        coupling = [
            jnp.where(step >= o, beta * ratio[o] * jnp.sum(dk * key_back[o], axis=1, keepdims=True), 0.0)
            for o in range(1, STEPS)
        ]
        update = beta_prior
        for _ in range(STEPS - 1):
            following = beta_prior
            for o in range(1, STEPS):
                following = following - coupling[o - 1] * shifted(update, o)
            update = following
        readout = whole * prior_q
        for o in range(STEPS):
            reach = jnp.sum(dq * key_back[o], axis=1, keepdims=True)
            readout = readout + jnp.where(step >= o, ratio[o] * reach, 0.0) * shifted(update, o)
        readout = readout * (128 ** -0.5)

        def normal(x):
            return x * lax.rsqrt(jnp.mean(x * x, axis=1, keepdims=True) + norm_eps) * dgain[...]

        normalized = jnp.concatenate([normal(readout[:, :128]), normal(readout[:, 128:])], axis=1)
        normalized = (normalized * zgate * jax.nn.sigmoid(zgate)).astype(bf16)

        total = dot(normalized, wdo[...])
        for e in range(GROUP):
            d_out[:, e] = total[:, e * SHARE : (e + 1) * SHARE].astype(bf16).reshape(2, ROWS, SHARE)
        for n, offset in enumerate(FAR_FIRST):
            other = peer(offset)
            send(d_out.at[0, other], d_in.at[n], 4, (back, other))
            send(d_out.at[1, other], d_in.at[n], 4, (front, other))
        send(d_out.at[0, me], d_in.at[GROUP - 1], 4, (back, me))
        result = stream[ROWS:BOTH] + d_out[1, me].astype(f32)
        sent(m_in.at[pl.ds(0, GROUP - 1), 0], 0)
        sent(s_more, 5)
        sent(a_in, 2)
        sent(x_in.at[pl.ds(0, GROUP - 1)], 3)
        sent(base_out, 10)
        arrived(d_in.at[pl.ds(0, GROUP - 1)], 4)
        for n in range(GROUP - 1):
            result = result + d_in[n].astype(f32)
        out_ref[...] = result
        sent(d_out.at[0], 4)
        sent(d_out.at[1, pl.ds(0, GROUP - 1)], 4)


def body(
    kv_pool, page_owner, page_slot, lengths, queries, gates, new_kv, tokens, attn_gain, out_heads,
    w_query_key, w_value_gate, w_beta_decay, decay_scale, dt_bias, delta_gain, w_delta_out, prior_state,
):
    hbm = pl.BlockSpec(memory_space=pl.ANY)
    smem = pl.BlockSpec(memory_space=pltpu.SMEM)
    vmem = pltpu.VMEM
    operands = (
        (kv_pool.reshape(SLOTS, 2, PAGE, KVH * HD), hbm),
        (page_owner, hbm),
        (page_slot, hbm),
        (lengths.reshape(REQS), smem),
        (queries.reshape(ROWS * GROUP, HD), hbm),
        (gates.reshape(ROWS, GROUP, HD), hbm),
        (new_kv.reshape(ROWS, 2, KVH, HD), hbm),
        (tokens, hbm),
        (attn_gain.reshape(1, D), hbm),
        (out_heads.reshape(HD, D), hbm),
        (w_query_key.reshape(2 * D, 128), hbm),
        (w_value_gate.reshape(4 * D, 128), hbm),
        (w_beta_decay.transpose(1, 2, 0), hbm),
        (decay_scale, smem),
        (dt_bias, smem),
        (delta_gain.reshape(1, 128), hbm),
        (w_delta_out.reshape(2 * 128, D), hbm),
        (prior_state, hbm),
    )
    out = pl.pallas_call(
        kernel,
        out_shape=jax.ShapeDtypeStruct((ROWS, SHARE), f32),
        in_specs=[spec for _, spec in operands],
        out_specs=pl.BlockSpec(memory_space=pltpu.VMEM),
        scratch_shapes=[
            vmem((KVH, 2, SLOTS, PAGE, HD), f32),
            vmem((REQS, 1, PAGES), jnp.int32),
            vmem((REQS, 1, PAGES), jnp.int32),
            vmem((2, ROWS * GROUP, 128), f32),
            vmem((ROWS, GROUP, HD), bf16),
            vmem((ROWS, 2, KVH, HD), f32),
            vmem((2, REQS, STEPS, SHARE), bf16),
            vmem((1, D), f32),
            vmem((HD, D), bf16),
            vmem((2 * D, 128), bf16),
            vmem((4 * D, 128), bf16),
            vmem((2, 2, D), bf16),
            vmem((1, 128), f32),
            vmem((2 * 128, D), bf16),
            vmem((REQS, GROUP, 2, 8, 128), f32),
            vmem((512, 128), f32),
            vmem((1024, 128), f32),
            vmem((D, 6 * 128), bf16),
            vmem((8, D), f32),
            vmem((GROUP, 64, 128), bf16),
            vmem((GROUP, 64, 128), bf16),
            vmem((GROUP, 2, 64, 128), bf16),
            vmem((2 * REQS, 256, 128), bf16),
            vmem((GROUP, ROWS, MSG), bf16),
            vmem((GROUP + 1, 2, ROWS, MSG), bf16),
            vmem((ROWS, MSG), bf16),
            vmem((ROWS, HD), bf16),
            vmem((ROWS, HD), bf16),
            vmem((GROUP, BOTH, SHARE), bf16),
            vmem((GROUP - 1, BOTH, SHARE), bf16),
            vmem((BOTH, SHARE), bf16),
            vmem((GROUP, BOTH, SHARE), bf16),
            vmem((2, GROUP, ROWS, SHARE), bf16),
            vmem((GROUP, ROWS, SHARE), bf16),
            vmem((ROWS, SHARE), f32),
            vmem((ROWS, SHARE), f32),
            pltpu.SemaphoreType.DMA((20,)),
            pltpu.SemaphoreType.DMA((11,)),
            pltpu.SemaphoreType.DMA((11,)),
            pltpu.SemaphoreType.REGULAR,
            pltpu.SemaphoreType.REGULAR,
        ],
        compiler_params=pltpu.CompilerParams(
            collective_id=0, has_side_effects=True, vmem_limit_bytes=60 * 1024 * 1024
        ),
    )(*[value for value, _ in operands])
    return out.reshape(REQS, 1, STEPS, SHARE)


def solution(mesh):
    return jax.shard_map(
        body,
        mesh=mesh,
        in_specs=(
            P("req", "seq", None, None, None),
            P(None, "req", None),
            P(None, "req", None),
            P(None, "req"),
            P(None, "req", None, None, None),
            P(None, "req", None, None, None),
            P(None, "req", None, None, None, None),
            P(None, "req", None, None),
            P(),
            P("seq", None, None),
            P(None, "seq", None, None),
            P(None, "seq", None, None),
            P(None, None, "seq"),
            P("seq"),
            P("seq"),
            P(),
            P("seq", None, None),
            P(None, None, "req", "seq", None),
        ),
        out_specs=P(None, "req", None, "seq"),
        check_vma=False,
    )
```

time: 31.8 us -> 31.7 us (level)
  no operation moved by 1% of the time
where the time goes in v2:
time: 31.7 us; the launch traced here: 31.5 us
  Pallas kernels  30.2 us (95%)
  local copies, waits for them, and re-layouts  1.3 us (4%)
    pallas_call x1, Pallas kernels, body(): pl.pallas_call(kernel, out_shape=jax.ShapeDtypeStruct((ROWS, SHARE), f32)...  30.2 us
    unnamed x1, local copies, waits for them, and re-layouts  1.3 us

profile of v2, /device:TPU:1, one launch (start us, length us, event | category | flops | bytes accessed | tf_op | source)
XLA Modules:
  0.0 31.5 jit_solution(696693368188179986)
XLA Ops:
  0.0 30.2 %shard_map.172 = f32[16,128]{1,0:T(8,128)} custom-call(f32[48,2,16,512]{3,2,1,0:T(8,128)} %bitcast.15, s32[4,1,192]{2,1,0:T(1,128)} %owner_hbm.1, s32[4,1,192]{2,1,0:T(1,128)} %slot_hbm.1, s32[4]{0:T(128)} %bitcast.26, f32[256,256]{1,0:T(8,128)} %bitcast.20, bf16[16,16,256]{2,1,0:T(8,128)(2,1)} %bitcast.21, f32[16,2,2,256]{3,2,1,0:T(2,128)} %bitcast.22, ...), custom_call_target="tpu_custom_call" | custom-call | tf_op jit(solution)/shard_map/pallas_call | solution.py:510
  30.2 1.3 %copy.21 = f32[4,1,4,128]{3,2,1,0:T(4,128)} copy(f32[4,1,4,128]{3,2,1,0:T(4,128)} %bitcast.23) | data formatting | bytes 16384

commit v3 on v2

--- a/solution.py
+++ b/solution.py
@@ -30,6 +30,7 @@
 OFFSETS = [(y, x) for y in range(4) for x in range(4) if y or x]
 FAR_FIRST = sorted(OFFSETS, key=lambda o: -(min(o[0], 4 - o[0]) + min(o[1], 4 - o[1])))
 PLACES = (1, 0, 3, 2, 6, 5, 7, 4)
+ORDER = (1, 0, 3, 2, 7, 5, 4, 6)
 
 
 def dot(a, b):
@@ -55,7 +56,7 @@
     kv, owner, slot, q, gates, new, tokens, gain, wo, wqk, wvg, wmix, dgain, wdo, state,
     fq, fv, w_all, w_mix, s_out, s_more, s_in, held_states, m_out, m_in, draft_out, gate_out, gate_in,
     a_out, a_in, x_out, x_in, d_out, d_in, base_out, base_in,
-    load_sem, send_sem, recv_sem, ready_sem, go_sem,
+    load_sem, send_sem, recv_sem, ready_sem,
 ):
     i = lax.axis_index("req")
     me = lax.axis_index("seq")
@@ -103,9 +104,6 @@
         for d in range(GROUP):
             use((2 * (me // 2), lax.rem(me + d, GROUP)))
 
-    for offset in FAR_FIRST:
-        greet((front, peer(offset)))
-
     @pl.when(on_back)
     def _():
         greet((front, me))
@@ -114,12 +112,19 @@
     def _():
         for offset in FAR_FIRST:
             greet((back, peer(offset)))
+            greet((front, peer(offset)))
         greet((back, me))
 
-    early_receiver = on_front & (my_rank <= rank(me // 2))
+    early_receiver = on_front & (my_rank < rank(me // 2))
+    own_receiver = on_front & (z == me // 2)
     late_receiver = on_front & (my_rank > rank(me // 2))
 
     @pl.when(early_receiver)
+    def _():
+        for d in range(GROUP):
+            greet((me, lax.rem(me + d, GROUP)))
+
+    @pl.when(own_receiver)
     def _():
         each_state_source(greet)
 
@@ -204,8 +209,8 @@
         barrier,
         jnp.where(
             on_front,
-            2 * GROUP - 1 + GROUP * late_receiver.astype(jnp.int32),
-            GROUP + 2 * (my_rank + 1),
+            GROUP + my_rank + GROUP * late_receiver.astype(jnp.int32),
+            GROUP + my_rank + 2,
         ),
     )
 
@@ -238,7 +243,7 @@
     def _():
         each_state_source(
             lambda source: pl.semaphore_signal(
-                ready_sem, inc=1, device_id=source, device_id_type=MESH
+                ready_sem.at[z], inc=1, device_id=source, device_id_type=MESH
             )
         )
 
@@ -280,34 +285,39 @@
     for g in range(GROUP):
         s_out[g] = state[:, g].reshape(REQS * 2 * 8, 128).astype(bf16)
 
+    def send_states(src, c, phase_sent, chosen):
+        for d in range(LEVELS):
+            level = lax.rem(z + me + LEVELS - d, LEVELS)
+
+            @pl.when(chosen(rank(level)))
+            def _():
+                send(src.at[pl.ds(2 * level, 2)], s_in.at[me], 1, (2 * level + 1, 2 * z + c), phase_sent)
+
     @pl.when(on_back)
     def _():
-        def send_states(c, chosen):
-            for d in range(LEVELS):
-                level = lax.rem(z + me + LEVELS - d, LEVELS)
-
-                @pl.when(chosen(rank(level)))
-                def _():
+        send_states(s_out, 0, 1, lambda place: place <= my_rank)
+        arrived(s_more, 5)
+        send_states(s_more, 1, 6, lambda place: place == my_rank)
+
+        for r, level in enumerate(ORDER):
+            @pl.when(my_rank < r)
+            def _():
+                pl.semaphore_wait(ready_sem.at[level], 2)
+                for c in range(2):
                     send(
-                        (s_out, s_more)[c].at[pl.ds(2 * level, 2)], s_in.at[me], 1, (2 * level + 1, 2 * z + c)
+                        (s_out, s_more)[c].at[pl.ds(2 * level, 2)], s_in.at[me], 1, (2 * level + 1, 2 * z + c), (1, 6)[c]
                     )
 
-        send_states(0, lambda place: place <= my_rank)
-        arrived(s_more, 5)
-        send_states(1, lambda place: place <= my_rank)
-
-        @pl.when(my_rank < LEVELS - 1)
-        def _():
-            pl.semaphore_wait(ready_sem, 2 * (LEVELS - 1 - my_rank))
-
-        pl.semaphore_wait(go_sem, 1)
-        for c in range(2):
-            send_states(c, lambda place: place > my_rank)
         sent(s_out, 1)
-        sent(s_more, 1)
+        for r in range(LEVELS):
+
+            @pl.when(my_rank == r)
+            def _():
+                sent(s_more.at[pl.ds(0, 2 * (LEVELS - r))], 6)
 
     @pl.when(on_front)
     def _():
+        send_states(s_out, 1, 1, lambda place: place < my_rank)
         send(s_out, s_more, 5, (back, me))
 
     @pl.when(on_back)
@@ -352,7 +362,6 @@
         gate = jax.nn.sigmoid(jnp.concatenate([gate_in[...], gate_out[...]], axis=0).astype(f32))
 
         arrived(m_in.at[pl.ds(0, GROUP)], 0)
-        pl.semaphore_signal(go_sem, inc=1, device_id=(back, me), device_id_type=MESH)
         parts = [m_in[n].reshape(BOTH, MSG) for n in range(GROUP + 1)]
         ceiling = parts[0][:, HD : HD + 1].astype(f32)
         for part in parts[1:]:
@@ -469,6 +478,12 @@
         result = stream[ROWS:BOTH] + d_out[1, me].astype(f32)
         sent(m_in.at[pl.ds(0, GROUP - 1), 0], 0)
         sent(s_more, 5)
+        for r in range(1, LEVELS):
+
+            @pl.when(my_rank == r)
+            def _():
+                sent(s_out.at[pl.ds(0, 2 * r)], 1)
+
         sent(a_in, 2)
         sent(x_in.at[pl.ds(0, GROUP - 1)], 3)
         sent(base_out, 10)
@@ -552,8 +567,7 @@
             pltpu.SemaphoreType.DMA((20,)),
             pltpu.SemaphoreType.DMA((11,)),
             pltpu.SemaphoreType.DMA((11,)),
-            pltpu.SemaphoreType.REGULAR,
-            pltpu.SemaphoreType.REGULAR,
+            pltpu.SemaphoreType.REGULAR((LEVELS,)),
         ],
         compiler_params=pltpu.CompilerParams(
             collective_id=0, has_side_effects=True, vmem_limit_bytes=60 * 1024 * 1024

time: 31.7 us -> 31.3 us (0.987)
  Pallas kernels: 30.2 us -> 29.8 us
    pallas_call x1, Pallas kernels: 30.2 us -> 29.8 us  [body(): pl.pallas_call(kernel, out_shape=jax.ShapeDtypeStruct((ROWS, SHARE), f32)...]
where the time goes in v3:
time: 31.3 us; the launch traced here: 31.1 us
  Pallas kernels  29.8 us (95%)
  local copies, waits for them, and re-layouts  1.3 us (4%)
    pallas_call x1, Pallas kernels, body(): pl.pallas_call(kernel, out_shape=jax.ShapeDtypeStruct((ROWS, SHARE), f32)...  29.8 us
    unnamed x1, local copies, waits for them, and re-layouts  1.3 us

profile of v3, /device:TPU:1, one launch (start us, length us, event | category | flops | bytes accessed | tf_op | source)
XLA Modules:
  0.0 31.1 jit_solution(1118484451650645396)
XLA Ops:
  0.0 29.8 %shard_map.172 = f32[16,128]{1,0:T(8,128)} custom-call(f32[48,2,16,512]{3,2,1,0:T(8,128)} %bitcast.15, s32[4,1,192]{2,1,0:T(1,128)} %owner_hbm.1, s32[4,1,192]{2,1,0:T(1,128)} %slot_hbm.1, s32[4]{0:T(128)} %bitcast.26, f32[256,256]{1,0:T(8,128)} %bitcast.20, bf16[16,16,256]{2,1,0:T(8,128)(2,1)} %bitcast.21, f32[16,2,2,256]{3,2,1,0:T(2,128)} %bitcast.22, ...), custom_call_target="tpu_custom_call" | custom-call | tf_op jit(solution)/shard_map/pallas_call | solution.py:525
  29.8 1.3 %copy.21 = f32[4,1,4,128]{3,2,1,0:T(4,128)} copy(f32[4,1,4,128]{3,2,1,0:T(4,128)} %bitcast.23) | data formatting | bytes 16384

commit v4 on v3

--- a/solution.py
+++ b/solution.py
@@ -287,7 +287,7 @@
 
     def send_states(src, c, phase_sent, chosen):
         for d in range(LEVELS):
-            level = lax.rem(z + me + LEVELS - d, LEVELS)
+            level = lax.rem(z + me + d, LEVELS)
 
             @pl.when(chosen(rank(level)))
             def _():
@@ -401,12 +401,13 @@
                 blocks = [rows[j, h] for h in range(2) for j in range(GROUP)]
                 held_states[g * REQS + r] = jnp.concatenate(blocks, axis=0).astype(bf16)
 
+        inverse = 1.0 / gain[...]
         arrived(x_in.at[pl.ds(0, GROUP - 1)], 3)
         y = jnp.concatenate([x_in[e] for e in range(GROUP)], axis=1)
         proj = dot(y, w_all[...])
         y = y.astype(f32)
         mixes = [jnp.sum(y * w_mix[c : c + 1], axis=1, keepdims=True) for c in range(4)]
-        x = y / gain[...]
+        x = y * inverse
         squares = jnp.sum(x * x, axis=1, keepdims=True)
         scale = lax.rsqrt(squares * (1.0 / D) + norm_eps)
         proj = proj * scale
@@ -472,8 +473,10 @@
             d_out[:, e] = total[:, e * SHARE : (e + 1) * SHARE].astype(bf16).reshape(2, ROWS, SHARE)
         for n, offset in enumerate(FAR_FIRST):
             other = peer(offset)
+            send(d_out.at[1, other], d_in.at[n], 4, (front, other))
+        for n, offset in enumerate(FAR_FIRST):
+            other = peer(offset)
             send(d_out.at[0, other], d_in.at[n], 4, (back, other))
-            send(d_out.at[1, other], d_in.at[n], 4, (front, other))
         send(d_out.at[0, me], d_in.at[GROUP - 1], 4, (back, me))
         result = stream[ROWS:BOTH] + d_out[1, me].astype(f32)
         sent(m_in.at[pl.ds(0, GROUP - 1), 0], 0)

time: 31.3 us -> 30.7 us (0.981)
  Pallas kernels: 29.8 us -> 29.3 us
    pallas_call x1, Pallas kernels: 29.8 us -> 29.3 us  [body(): pl.pallas_call(kernel, out_shape=jax.ShapeDtypeStruct((ROWS, SHARE), f32)...]
where the time goes in v4:
time: 30.7 us; the launch traced here: 30.6 us
  Pallas kernels  29.3 us (95%)
  local copies, waits for them, and re-layouts  1.3 us (4%)
    pallas_call x1, Pallas kernels, body(): pl.pallas_call(kernel, out_shape=jax.ShapeDtypeStruct((ROWS, SHARE), f32)...  29.3 us
    unnamed x1, local copies, waits for them, and re-layouts  1.3 us

profile of v4, /device:TPU:1, one launch (start us, length us, event | category | flops | bytes accessed | tf_op | source)
XLA Modules:
  0.0 30.6 jit_solution(3681841988202749226)
XLA Ops:
  0.0 29.3 %shard_map.172 = f32[16,128]{1,0:T(8,128)} custom-call(f32[48,2,16,512]{3,2,1,0:T(8,128)} %bitcast.15, s32[4,1,192]{2,1,0:T(1,128)} %owner_hbm.1, s32[4,1,192]{2,1,0:T(1,128)} %slot_hbm.1, s32[4]{0:T(128)} %bitcast.26, f32[256,256]{1,0:T(8,128)} %bitcast.20, bf16[16,16,256]{2,1,0:T(8,128)(2,1)} %bitcast.21, f32[16,2,2,256]{3,2,1,0:T(2,128)} %bitcast.22, ...), custom_call_target="tpu_custom_call" | custom-call | tf_op jit(solution)/shard_map/pallas_call | solution.py:528
  29.3 1.3 %copy.21 = f32[4,1,4,128]{3,2,1,0:T(4,128)} copy(f32[4,1,4,128]{3,2,1,0:T(4,128)} %bitcast.23) | data formatting | bytes 16384

commit v5 on v4

--- a/solution.py
+++ b/solution.py
@@ -394,13 +394,6 @@
         base_out[...] = stream[0:ROWS]
         send(base_out, base_in, 10, (back, me))
 
-        arrived(s_in, 1)
-        for g in range(2):
-            for r in range(REQS):
-                rows = s_in[:, g, r * 16 : (r + 1) * 16].astype(f32).reshape(GROUP, 2, 8, 128)
-                blocks = [rows[j, h] for h in range(2) for j in range(GROUP)]
-                held_states[g * REQS + r] = jnp.concatenate(blocks, axis=0).astype(bf16)
-
         inverse = 1.0 / gain[...]
         arrived(x_in.at[pl.ds(0, GROUP - 1)], 3)
         y = jnp.concatenate([x_in[e] for e in range(GROUP)], axis=1)
@@ -430,6 +423,13 @@
             return jnp.exp(-decay_scale[h] * soft)
 
         decay = jnp.where(high, decay_of(1), decay_of(0))
+
+        arrived(s_in, 1)
+        for g in range(2):
+            for r in range(REQS):
+                rows = s_in[:, g, r * 16 : (r + 1) * 16].astype(f32).reshape(GROUP, 2, 8, 128)
+                blocks = [rows[j, h] for h in range(2) for j in range(GROUP)]
+                held_states[g * REQS + r] = jnp.concatenate(blocks, axis=0).astype(bf16)
 
         both = jnp.concatenate([dk, dq], axis=0).astype(bf16)
         row_of = lax.rem(iota((2 * BOTH, 2 * 128), 0) // STEPS, 2 * REQS)

time: 30.7 us -> 30.9 us (level)
  no operation moved by 1% of the time
where the time goes in v5:
time: 30.9 us; the launch traced here: 30.7 us
  Pallas kernels  29.4 us (95%)
  local copies, waits for them, and re-layouts  1.3 us (4%)
    pallas_call x1, Pallas kernels, body(): pl.pallas_call(kernel, out_shape=jax.ShapeDtypeStruct((ROWS, SHARE), f32)...  29.4 us
    unnamed x1, local copies, waits for them, and re-layouts  1.3 us

profile of v5, /device:TPU:1, one launch (start us, length us, event | category | flops | bytes accessed | tf_op | source)
XLA Modules:
  0.0 30.7 jit_solution(477328920150077395)
XLA Ops:
  0.0 29.4 %shard_map.172 = f32[16,128]{1,0:T(8,128)} custom-call(f32[48,2,16,512]{3,2,1,0:T(8,128)} %bitcast.15, s32[4,1,192]{2,1,0:T(1,128)} %owner_hbm.1, s32[4,1,192]{2,1,0:T(1,128)} %slot_hbm.1, s32[4]{0:T(128)} %bitcast.26, f32[256,256]{1,0:T(8,128)} %bitcast.20, bf16[16,16,256]{2,1,0:T(8,128)(2,1)} %bitcast.21, f32[16,2,2,256]{3,2,1,0:T(2,128)} %bitcast.22, ...), custom_call_target="tpu_custom_call" | custom-call | tf_op jit(solution)/shard_map/pallas_call | solution.py:528
  29.5 1.3 %copy.21 = f32[4,1,4,128]{3,2,1,0:T(4,128)} copy(f32[4,1,4,128]{3,2,1,0:T(4,128)} %bitcast.23) | data formatting | bytes 16384
